TPU v7x, 32 devices: a whole 2x2x4 slice. The times are simulated.
32 devices in a mesh: groups: 2 (over x), vel: 8 (over z, y), sub: 2 (over core).
Axes of the slice: x: 2, y: 2, z: 4, core: 2. Of those that a mesh axis runs over, the one named last changes fastest.
Arguments:
- dist: float32 [16, 256, 1024], P('sub', 'vel', 'groups'), parts along dimension 2, may hold values from 0 to 6, as said below
- cell_type: int32 [1024], P('groups'), parts along dimension 0, may hold values from 0 to 1, as said below
- groove_mask: int32 [64], P('groups'), parts along dimension 0, may hold values 0 or 1
Outputs:
- dist_next: float32 [16, 256, 1024], P('sub', 'vel', 'groups'), parts along dimension 2
There are 2 independent parts, one for each index of `groups`. A program takes and returns all parts, laid end to end along the dimension named above; each array names one. Nothing has to cross between parts.
Inputs may be any that keep to these rules, and one draw needn't show every extreme that they name: `cell_type`: in each column the solid cells are its lowest ones; a column holds at most a quarter of 16 of them, and every draw has columns with that many and columns with none; grooves repeat along the columns with a period of 4 to 12 columns. `dist`: every entry is positive.
All inputs are finite; a program needn't handle non-finite values.
Results may differ from a plain program's by a relative error of at most 0.0001.
Values sent between devices are 32-bit elements; how exact they have to be, the bound alone decides.
A program may use at most 128 MiB of HBM per device.

v0:
```python
import math
import jax
import jax.numpy as jnp
from jax import lax
from jax.sharding import PartitionSpec as P

VN = 16
SY = 16
STEPS = 2
VEL_RANGE = 5.0
TOP_SPEED = 1.0
ACC_LAND = 0.4
ACC_TOP = 0.7
KNUDSEN = 1.0
HIGHEST = lax.Precision.HIGHEST
FORMS = ("kj,jxzc->kxzc", "kj,yjzc->ykzc", "kj,yxjc->yxkc")


def swapped(value, axis, distance):
    mask = 2**distance
    pairs = [(source, source ^ mask) for source in range(lax.axis_size(axis))]
    return lax.ppermute(value, axis, pairs)


def spacing_of(count):
    return 2.0 * VEL_RANGE / count


def time_step(count):
    return 0.8 / ((count - 1) * spacing_of(count))


def speeds(index, count):
    return (index.astype(jnp.float32) - (count - 1) / 2.0) * spacing_of(count)


def wave_numbers(count):
    index = jnp.arange(count, dtype=jnp.int32)
    wrapped = jnp.where(index < count // 2, index, index - count)
    return wrapped.astype(jnp.float32) * (math.pi / VEL_RANGE)


def kernels(count):
    wave = wave_numbers(count)
    wave_y = wave[:, None, None]
    wave_x = wave[None, :, None]
    wave_z = wave[None, None, :]
    square = wave_y * wave_y + wave_x * wave_x + wave_z * wave_z
    first = 1.0 / (1.0 + square / 12.0)
    second = 3.0 * jnp.cos(0.9 * wave_x) / (1.0 + square / 10.0)
    damped = 1.0 + square / 9.0
    loss = 3.0 / (damped * damped)
    return (first, second, loss)


def dft_tables(count):
    index = jnp.arange(count, dtype=jnp.float32)
    angle = 2.0 * math.pi / count * index[:, None] * index[None, :]
    return (jnp.cos(angle), jnp.sin(angle))


def full_grid(count):
    index = jnp.arange(count * count * count, dtype=jnp.int32)
    velocity_y = speeds(index // (count * count), count)
    velocity_x = speeds(index // count % count, count)
    velocity_z = speeds(index % count, count)
    return (velocity_x, velocity_y, velocity_z)


def wall_tables(velocity_x, velocity_y, velocity_z):
    rest = jnp.exp(
        -(velocity_x * velocity_x + velocity_y * velocity_y + velocity_z * velocity_z) / 2.0
    )
    shifted = velocity_x - TOP_SPEED
    moving = jnp.exp(-(shifted * shifted + velocity_y * velocity_y + velocity_z * velocity_z) / 2.0)
    weights = jnp.stack(
        [
            jnp.maximum(-velocity_x, 0.0),
            jnp.maximum(velocity_x, 0.0),
            jnp.maximum(-velocity_y, 0.0),
            jnp.maximum(velocity_y, 0.0),
        ]
    )
    return (rest, moving, weights)


def wall_norms(count):
    velocity_x, velocity_y, velocity_z = full_grid(count)
    rest, moving, weights = wall_tables(velocity_x, velocity_y, velocity_z)
    return (
        jnp.sum(jnp.maximum(velocity_x, 0.0) * rest),
        jnp.sum(jnp.maximum(-velocity_x, 0.0) * rest),
        jnp.sum(jnp.maximum(velocity_y, 0.0) * rest),
        jnp.sum(jnp.maximum(-velocity_y, 0.0) * moving),
    )


def cell_masks(cell_type, groove_mask, height_count):
    total = cell_type.shape[0]
    solid = cell_type.astype(jnp.float32)
    height = jnp.arange(total, dtype=jnp.int32) % height_count
    left_solid = jnp.roll(solid, height_count)
    right_solid = jnp.roll(solid, -height_count)
    below_solid = jnp.where(height == 0, 1.0, jnp.roll(solid, 1))
    top_wall = jnp.where(height == height_count - 1, 1.0, 0.0 * solid)
    accommodation = jnp.repeat(jnp.where(groove_mask == 1, 1.0, ACC_LAND), height_count)
    return jnp.stack([left_solid, right_solid, below_solid, top_wall, accommodation, 1.0 - solid])


def advance(center, left, right, below, above, mirror, flux, masks, velocity, norms, step_size):
    velocity_x, velocity_y, rest, moving = velocity
    left_solid = masks[0][None, :]
    right_solid = masks[1][None, :]
    below_solid = masks[2][None, :]
    top_wall = masks[3][None, :]
    accommodation = masks[4][None, :]
    fluid = masks[5][None, :]
    left_ghost = (flux[0] / norms[0])[None, :] * rest
    right_ghost = (flux[1] / norms[1])[None, :] * rest
    below_ghost = (1.0 - accommodation) * mirror + accommodation * (flux[2] / norms[2])[
        None, :
    ] * rest
    above_ghost = (1.0 - ACC_TOP) * mirror + ACC_TOP * (flux[3] / norms[3])[None, :] * moving
    left_value = jnp.where(left_solid > 0.0, left_ghost, left)
    right_value = jnp.where(right_solid > 0.0, right_ghost, right)
    below_value = jnp.where(below_solid > 0.0, below_ghost, below)
    above_value = jnp.where(top_wall > 0.0, above_ghost, above)
    change = jnp.maximum(velocity_x, 0.0) * (center - left_value) + jnp.minimum(velocity_x, 0.0) * (
        right_value - center
    )
    change = (
        change
        + jnp.maximum(velocity_y, 0.0) * (center - below_value)
        + jnp.minimum(velocity_y, 0.0) * (above_value - center)
    )
    return (center - step_size * change) * fluid


def fourier_pass(real_part, imag_part, cosine, sine_table, form, forward):

    def apply(table, values):
        return jnp.einsum(form, table, values, precision=HIGHEST)

    if imag_part is None:
        return (apply(cosine, real_part), -apply(sine_table, real_part))
    if forward:
        return (
            apply(cosine, real_part) + apply(sine_table, imag_part),
            apply(cosine, imag_part) - apply(sine_table, real_part),
        )
    return (
        apply(cosine, real_part) - apply(sine_table, imag_part),
        apply(cosine, imag_part) + apply(sine_table, real_part),
    )


def collide(cube, tables, cosine, sine_table, rate):
    count = cube.shape[0]
    scale = 1.0 / (count * count * count)
    real_part, imag_part = fourier_pass(cube, None, cosine, sine_table, FORMS[0], True)
    real_part, imag_part = fourier_pass(real_part, imag_part, cosine, sine_table, FORMS[1], True)
    real_part, imag_part = fourier_pass(real_part, imag_part, cosine, sine_table, FORMS[2], True)

    def inverse(table):
        factor = table[..., None]
        first_real, first_imag = fourier_pass(
            real_part * factor, imag_part * factor, cosine, sine_table, FORMS[0], False
        )
        second_real, second_imag = fourier_pass(
            first_real, first_imag, cosine, sine_table, FORMS[1], False
        )
        last = jnp.einsum(FORMS[2], cosine, second_real, precision=HIGHEST) - jnp.einsum(
            FORMS[2], sine_table, second_imag, precision=HIGHEST
        )
        return last * scale

    gain = inverse(tables[0]) * inverse(tables[1])
    return cube + rate * (gain - cube * inverse(tables[2]))


def local(dist, cell_type, groove_mask):
    count = VN
    height_count = SY
    volume = count * count * count
    local_y, local_xz, total_cells = dist.shape
    masks = cell_masks(cell_type, groove_mask, height_count)
    norms = wall_norms(count)
    step_size = time_step(count)
    rate = step_size / KNUDSEN
    cosine, sine_table = dft_tables(count)
    tables = kernels(count)
    sub_index = lax.axis_index("sub")
    vel_index = lax.axis_index("vel")
    index_y = sub_index * local_y + jnp.arange(local_y, dtype=jnp.int32)
    index_xz = vel_index * local_xz + jnp.arange(local_xz, dtype=jnp.int32)
    block_shape = (local_y, local_xz)
    velocity_y = jnp.broadcast_to(speeds(index_y, count)[:, None], block_shape).reshape(-1)
    velocity_x = jnp.broadcast_to(speeds(index_xz // count, count)[None, :], block_shape).reshape(
        -1
    )
    velocity_z = jnp.broadcast_to(speeds(index_xz % count, count)[None, :], block_shape).reshape(-1)
    rest, moving, weights = wall_tables(velocity_x, velocity_y, velocity_z)
    velocity = (velocity_x[:, None], velocity_y[:, None], rest[:, None], moving[:, None])
    columns_total = total_cells // height_count
    depth = jnp.sum(cell_type.reshape(columns_total, height_count), axis=1)
    bottom_index = jnp.arange(columns_total, dtype=jnp.int32) * height_count + depth
    state = dist
    for iteration in range(STEPS):
        space = lax.all_to_all(
            lax.all_to_all(state, "vel", split_axis=2, concat_axis=1, tiled=True),
            "sub",
            split_axis=2,
            concat_axis=0,
            tiled=True,
        )
        cells = space.shape[2]
        post = collide(
            space.reshape(count, count, count, cells), tables, cosine, sine_table, rate
        ).reshape(volume, cells)
        back = lax.all_to_all(
            lax.all_to_all(
                post.reshape(count, count * count, 1, cells),
                "vel",
                split_axis=1,
                concat_axis=2,
                tiled=True,
            ),
            "sub",
            split_axis=0,
            concat_axis=3,
            tiled=True,
        )
        center = back.reshape(local_y * local_xz, total_cells)
        flux = lax.psum(jnp.dot(weights, center, precision=HIGHEST), ("vel", "sub"))
        shaped = center.reshape(local_y, local_xz, total_cells)
        bottom_rows = jnp.take(shaped, bottom_index, axis=2)
        top_rows = shaped[:, :, height_count - 1 :: height_count]
        outgoing = jnp.where(sub_index == 0, bottom_rows, top_rows)
        incoming = swapped(outgoing, "sub", 0)
        mirror = jnp.repeat(incoming[::-1], height_count, axis=2).reshape(
            local_y * local_xz, total_cells
        )
        result = advance(
            center,
            jnp.roll(center, height_count, 1),
            jnp.roll(center, -height_count, 1),
            jnp.roll(center, 1, 1),
            jnp.roll(center, -1, 1),
            mirror,
            flux,
            masks,
            velocity,
            norms,
            step_size,
        )
        state = result.reshape(local_y, local_xz, total_cells)
    return state


def solution(mesh):
    return jax.shard_map(
        local,
        mesh=mesh,
        in_specs=(P("sub", "vel", "groups"), P("groups"), P("groups")),
        out_specs=P("sub", "vel", "groups"),
        check_vma=False,
    )
```

profile of v0, /device:TPU:1, one launch (start us, length us, event | category | flops | bytes accessed | tf_op | source)
XLA Modules:
  0.0 529.2 jit_solution(7535001363961206787)
XLA Ops:
  3.6 6.4 %all-to-all-start = ((f32[8,1,16384]{2,1,0:T(1,128)}), f32[8,1,16384]{2,1,0:T(1,128)S(1)}, u32[]{:S(2)}, u32[]{:S(2)}) async-start(f32[8,1,16384]{2,1,0:T(1,128)} %reshape.613), calls=%async_computation | async-start | bytes 1048576 | tf_op jit(solution)/shard_map/all_to_all | solution.py:210
  19.5 3.9 all-to-all-done
  27.4 5.8 %all_to_all.132 = f32[8,256,64]{1,0,2:T(8,128)S(1)} all-to-all(f32[8,256,64]{1,0,2:T(8,128)S(1)} %copy.780), channel_id=1, replica_groups=mesh['groups'=2,'vel'=8,'sub'=2] {'sub'}, dimensions={2} | all-to-all | bytes 1048576 | tf_op jit(solution)/shard_map/all_to_all | solution.py:209
  38.6 3.3 fusion.158
  41.9 3.3 fusion.160
  45.2 3.5 subtract_bitcast_fusion.7
  53.7 3.4 add_bitcast_fusion.7
  60.0 3.4 multiply_bitcast_fusion.10
  72.4 3.4 fusion.134
  75.8 3.3 fusion.136
  88.1 3.4 fusion.102
  91.4 3.7 fusion.104
  103.9 3.5 fusion.118
  107.4 3.3 fusion.120
  113.7 3.3 subtract_bitcast_fusion.6
  117.1 3.5 add_bitcast_fusion.6
  128.6 3.8 subtract_bitcast_fusion.4
  132.4 3.4 add_bitcast_fusion.4
  144.0 3.4 subtract_bitcast_fusion.5
  147.4 3.3 add_bitcast_fusion.5
  155.9 8.6 %fusion.5 = f32[16,16,16,32]{3,0,2,1:T(8,128)} fusion(f32[16,16,16,32]{3,0,2,1:T(8,128)S(1)} %bitcast.348, f32[16,16,32,16]{2,3,1,0:T(8,128)S(1)} %fusion.23, f32[16,16,32,16]{2,3,1,0:T(8,128)S(1)} %fusion.25, f32[16,16,32,16]{2,3,1,0:T(8,128)S(1)} %fusion.29, f32[16,16,32,16]{2,3,1,0:T(8,128)S(1)} %fusion.31, f32[16,16,32,16]{2,3,1,0:T(8,128)S(1)} %fusion.34, ...), kind=kLoop, calls=%fused_computation.9 | loop fusion | flops 1441792 | bytes 4194304 | tf_op jit(solution)/shard_map/add | solution.py:178
  167.7 3.9 all-to-all-start.2
  177.5 7.6 %all-to-all-done.2 = f32[8,1,16384]{2,1,0:T(1,128)S(1)} async-done(((f32[8,1,16384]{2,1,0:T(1,128)}), f32[8,1,16384]{2,1,0:T(1,128)S(1)}, u32[]{:S(2)}, u32[]{:S(2)}) %all-to-all-start.2) | async-done | bytes 524320 | tf_op jit(solution)/shard_map/all_to_all | solution.py:221
  192.3 5.5 %all_to_all.133 = f32[2,1,65536]{2,1,0:T(1,128)S(1)} all-to-all(f32[2,1,65536]{2,1,0:T(1,128)S(1)} %reshape.617), channel_id=1, replica_groups=mesh['groups'=2,'vel'=8,'sub'=2] {'sub'}, dimensions={0} | all-to-all | bytes 1048576 | tf_op jit(solution)/shard_map/all_to_all | solution.py:220
  217.9 30.5 %psum.14 = f32[4,512]{1,0:T(4,128)} all-reduce(f32[4,512]{1,0:T(4,128)} %fusion.572), channel_id=1, replica_groups=mesh['groups'=2,'vel'=8,'sub'=2] {'vel','sub'}, use_global_device_ids=true, to_apply=%region_0.1 | all-reduce | flops 2048 | bytes 16384 | tf_op jit(solution)/shard_map/psum | solution.py:234
  254.5 4.1 slice_divide_fusion.5
  269.2 3.3 fusion.253
  275.2 16.8 %all_to_all.134 = f32[8,1,16384]{2,1,0:T(1,128)S(1)} all-to-all(f32[8,1,16384]{2,1,0:T(1,128)S(1)} %reshape.619), channel_id=1, replica_groups=mesh['groups'=2,'vel'=8,'sub'=2] {'vel'}, dimensions={0} | all-to-all | bytes 1048576 | tf_op jit(solution)/shard_map/all_to_all | solution.py:210
  295.6 4.9 all_to_all.135
  305.8 3.3 fusion.94
  312.4 3.7 subtract_bitcast_fusion.3
  321.1 3.4 add_bitcast_fusion.3
  327.2 3.4 multiply_bitcast_fusion.4
  339.6 3.4 fusion.70
  349.2 3.3 fusion.48
  355.4 3.3 fusion.38
  358.8 3.5 fusion.40
  371.1 3.6 fusion.54
  380.9 3.3 subtract_bitcast_fusion.2
  384.3 3.7 add_bitcast_fusion.2
  396.0 3.6 subtract_bitcast_fusion
  399.6 3.4 add_bitcast_fusion
  411.2 3.4 subtract_bitcast_fusion.1
  414.6 3.3 add_bitcast_fusion.1
  423.3 8.6 %fusion.2 = f32[16,16,16,32]{3,0,2,1:T(8,128)} fusion(f32[16,16,16,32]{3,0,2,1:T(8,128)S(1)} %bitcast.345, f32[16,16,32,16]{2,3,1,0:T(8,128)S(1)} %fusion.7, f32[16,16,32,16]{2,3,1,0:T(8,128)S(1)} %fusion.9, f32[16,16,32,16]{2,3,1,0:T(8,128)S(1)} %fusion.13, f32[16,16,32,16]{2,3,1,0:T(8,128)S(1)} %fusion.15, f32[16,16,32,16]{2,3,1,0:T(8,128)S(1)} %fusion.18, ...), kind=kLoop, calls=%fused_computation.5 | loop fusion | flops 1441792 | bytes 4194304 | tf_op jit(solution)/shard_map/add | solution.py:178
  434.4 17.0 %all_to_all.136 = f32[8,1,16384]{2,1,0:T(1,128)S(1)} all-to-all(f32[8,1,16384]{2,1,0:T(1,128)S(1)} %reshape.621), channel_id=1, replica_groups=mesh['groups'=2,'vel'=8,'sub'=2] {'vel'}, dimensions={0} | all-to-all | bytes 1048576 | tf_op jit(solution)/shard_map/all_to_all | solution.py:221
  458.4 5.5 %all_to_all.137 = f32[2,1,65536]{2,1,0:T(1,128)S(1)} all-to-all(f32[2,1,65536]{2,1,0:T(1,128)S(1)} %reshape.623), channel_id=1, replica_groups=mesh['groups'=2,'vel'=8,'sub'=2] {'sub'}, dimensions={0} | all-to-all | bytes 1048576 | tf_op jit(solution)/shard_map/all_to_all | solution.py:220
  481.6 29.9 %psum.15 = f32[4,512]{1,0:T(4,128)S(1)} all-reduce(f32[4,512]{1,0:T(4,128)S(1)} %fusion.571), channel_id=1, replica_groups=mesh['groups'=2,'vel'=8,'sub'=2] {'vel','sub'}, use_global_device_ids=true, to_apply=%region_6.8 | all-reduce | flops 2048 | bytes 16384 | tf_op jit(solution)/shard_map/psum | solution.py:234
  (243 shorter events, 255.7 us)
Async XLA Ops:
  1.8 11.1 %copy-start.33 = (s32[32]{0:T(128)S(1)}, s32[32]{0:T(128)}, u32[]{:S(2)}) copy-start(s32[32]{0:T(128)} %param.7) | copy-start | bytes 388
  1.8 11.1 %copy-start.12 = (s32[512]{0:T(512)S(1)}, s32[512]{0:T(512)}, u32[]{:S(2)}) copy-start(s32[512]{0:T(512)} %param.6) | copy-start | bytes 6148
  3.6 19.8 %all-to-all-start = ((f32[8,1,16384]{2,1,0:T(1,128)}), f32[8,1,16384]{2,1,0:T(1,128)S(1)}, u32[]{:S(2)}, u32[]{:S(2)}) async-start(f32[8,1,16384]{2,1,0:T(1,128)} %reshape.613), calls=%async_computation | async-start | bytes 1048576 | tf_op jit(solution)/shard_map/all_to_all | solution.py:210
  10.5 8.9 %copy-start.23 = (f32[8]{0:T(128)}, f32[8]{0:T(128)S(1)}, u32[]{:S(2)}) copy-start(f32[8]{0:T(128)S(1)} %get-tuple-element.71) | copy-start | bytes 100
  12.9 6.5 %copy-start.24 = (f32[32]{0:T(128)}, f32[32]{0:T(128)S(1)}, u32[]{:S(2)}) copy-start(f32[32]{0:T(128)S(1)} %get-tuple-element.67) | copy-start | bytes 388
  17.3 251.8 %copy-start.13 = (f32[512]{0:T(512)}, f32[512]{0:T(512)S(1)}, u32[]{:S(2)}) copy-start(f32[512]{0:T(512)S(1)} %sub.287) | copy-start | bytes 6148
  164.5 9.8 %copy-start.21 = (f32[496]{0:T(512)S(1)}, f32[496]{0:T(512)}, u32[]{:S(2)}) copy-start(f32[496]{0:T(512)} %get-tuple-element.55) | copy-start | bytes 5956
  164.5 9.8 %copy-start.22 = (f32[496]{0:T(512)S(1)}, f32[496]{0:T(512)}, u32[]{:S(2)}) copy-start(f32[496]{0:T(512)} %get-tuple-element.56) | copy-start | bytes 5956
  164.5 9.8 %copy-start.26 = (f32[16]{0:T(128)S(1)}, f32[16]{0:T(128)}, u32[]{:S(2)}) copy-start(f32[16]{0:T(128)} %get-tuple-element.53) | copy-start | bytes 196
  164.5 9.8 %copy-start.27 = (f32[16]{0:T(128)S(1)}, f32[16]{0:T(128)}, u32[]{:S(2)}) copy-start(f32[16]{0:T(128)} %get-tuple-element.54) | copy-start | bytes 196
  164.5 10.5 %copy-start.32 = (s32[32]{0:T(128)S(1)}, s32[32]{0:T(128)}, u32[]{:S(2)}) copy-start(s32[32]{0:T(128)} %get-tuple-element.11) | copy-start | bytes 388
  164.5 12.9 %copy-start.28 = (f32[8]{0:T(128)S(1)}, f32[8]{0:T(128)}, u32[]{:S(2)}) copy-start(f32[8]{0:T(128)} %get-tuple-element.72) | copy-start | bytes 100
  164.5 12.9 %copy-start.29 = (f32[32]{0:T(128)S(1)}, f32[32]{0:T(128)}, u32[]{:S(2)}) copy-start(f32[32]{0:T(128)} %get-tuple-element.63) | copy-start | bytes 388
  164.5 12.9 %copy-start.30 = (f32[32]{0:T(128)S(1)}, f32[32]{0:T(128)}, u32[]{:S(2)}) copy-start(f32[32]{0:T(128)} %get-tuple-element.64) | copy-start | bytes 388
  164.6 12.9 %copy-start.31 = (f32[32]{0:T(128)S(1)}, f32[32]{0:T(128)}, u32[]{:S(2)}) copy-start(f32[32]{0:T(128)} %get-tuple-element.68) | copy-start | bytes 388
  167.7 17.5 %all-to-all-start.2 = ((f32[8,1,16384]{2,1,0:T(1,128)}), f32[8,1,16384]{2,1,0:T(1,128)S(1)}, u32[]{:S(2)}, u32[]{:S(2)}) async-start(f32[8,1,16384]{2,1,0:T(1,128)} %reshape.615), calls=%async_computation.2 | async-start | bytes 1048576 | tf_op jit(solution)/shard_map/all_to_all | solution.py:221
  177.5 91.6 %copy-start.8 = (f32[8,32]{1,0:T(8,128)}, f32[8,32]{1,0:T(8,128)S(1)}, u32[]{:S(2)}) copy-start(f32[8,32]{1,0:T(8,128)S(1)} %get-tuple-element.57) | copy-start | bytes 3076
  177.5 91.6 %copy-start.10 = (f32[8,32]{1,0:T(8,128)}, f32[8,32]{1,0:T(8,128)S(1)}, u32[]{:S(2)}) copy-start(f32[8,32]{1,0:T(8,128)S(1)} %get-tuple-element.58) | copy-start | bytes 3076
  208.0 2.7 copy-start.1
  249.8 15.5 %copy-start.7 = (f32[256,496]{0,1:T(8,128)S(1)}, f32[256,496]{0,1:T(8,128)}, u32[]{:S(2)}) copy-start(f32[256,496]{0,1:T(8,128)} %get-tuple-element.33) | copy-start | bytes 1523716
  249.8 16.5 %copy-start.5 = (f32[256,511]{0,1:T(8,128)S(1)}, f32[256,511]{0,1:T(8,128)}, u32[]{:S(2)}) copy-start(f32[256,511]{0,1:T(8,128)} %get-tuple-element.30) | copy-start | bytes 1569796
  250.9 16.4 %copy-start.4 = (f32[256,511]{0,1:T(8,128)S(1)}, f32[256,511]{0,1:T(8,128)}, u32[]{:S(2)}) copy-start(f32[256,511]{0,1:T(8,128)} %get-tuple-element.31) | copy-start | bytes 1569796
  251.9 16.4 %collective-permute-start = (f32[8,32,32]{2,1,0:T(8,128)S(1)}, f32[8,32,32]{2,1,0:T(8,128)S(1)}, u32[]{:S(2)}, u32[]{:S(2)}) collective-permute-start(f32[8,32,32]{2,1,0:T(8,128)S(1)} %bitcast_select_fusion.1), channel_id=1, source_target_pairs={{0,1},{1,0},{2,3},{3,2},{4,5},{5,4},{6,7},{7,6},{8,9},{9,8},{10,11... | collective-permute-start | bytes 98312 | tf_op jit(solution)/shard_map/ppermute | solution.py:22
  472.1 2.2 copy-start.17
  472.1 2.2 copy-start.18
  472.1 2.2 copy-start.19
  472.1 2.2 copy-start.20
  474.8 2.1 copy-start
  479.6 32.0 %copy-start.16 = (f32[1,512]{1,0:T(1,128)S(1)}, f32[1,512]{1,0:T(1,128)}, u32[]{:S(2)}) copy-start(f32[1,512]{1,0:T(1,128)} %stack_reshape.3) | copy-start | bytes 6148
  479.6 36.1 %copy-start.25 = (pred[32]{0:T(512)(128)(4,1)S(1)}, pred[32]{0:T(512)(128)(4,1)}, u32[]{:S(2)}) copy-start(pred[32]{0:T(512)(128)(4,1)} %get-tuple-element.10) | copy-start | bytes 100
  515.5 6.3 %copy-start.6 = (f32[256,496]{0,1:T(8,128)S(1)}, f32[256,496]{0,1:T(8,128)}, u32[]{:S(2)}) copy-start(f32[256,496]{0,1:T(8,128)} %get-tuple-element.27) | copy-start | bytes 1523716
  515.5 7.3 %copy-start.3 = (f32[256,511]{0,1:T(8,128)S(1)}, f32[256,511]{0,1:T(8,128)}, u32[]{:S(2)}) copy-start(f32[256,511]{0,1:T(8,128)} %get-tuple-element.24) | copy-start | bytes 1569796
  515.7 8.2 %copy-start.2 = (f32[256,511]{0,1:T(8,128)S(1)}, f32[256,511]{0,1:T(8,128)}, u32[]{:S(2)}) copy-start(f32[256,511]{0,1:T(8,128)} %get-tuple-element.25) | copy-start | bytes 1569796
  515.7 9.2 %collective-permute-start.1 = (f32[8,32,32]{2,1,0:T(8,128)S(1)}, f32[8,32,32]{2,1,0:T(8,128)S(1)}, u32[]{:S(2)}, u32[]{:S(2)}) collective-permute-start(f32[8,32,32]{2,1,0:T(8,128)S(1)} %bitcast_select_fusion), channel_id=1, source_target_pairs={{0,1},{1,0},{2,3},{3,2},{4,5},{5,4},{6,7},{7,6},{8,9},{9,8},{10,11... | collective-permute-start | bytes 98312 | tf_op jit(solution)/shard_map/ppermute | solution.py:22
  525.0 0.8 copy-start.9
  525.0 0.8 copy-start.11
  525.1 0.8 copy-start.14
  525.1 0.8 copy-start.15
where the time goes:
time: 535 us; the launch traced here: 529 us
  matrix products  244 us (46%)
  blocking collectives  116 us (22%)
  local copies, waits for them, and re-layouts  86.8 us (16%)
  other arithmetic  53.3 us (10%)
  starting transfers between devices  15.7 us (3%)
  waiting for transfers between devices  11.5 us (2%)
    dot_general x68, matrix products, apply(): return jnp.einsum(form, table, values, precision=HIGHEST)  212 us
    psum x2, blocking collectives, local(): flux = lax.psum(jnp.dot(weights, center, precision=HIGHEST), ('vel', 'sub'))  60.4 us
    unnamed x83, local copies, waits for them, and re-layouts  20 us
    add x2, other arithmetic, collide(): return cube + rate * (gain - cube * inverse(tables[2]))  17.1 us
    all_to_all x1, blocking collectives, local(): lax.all_to_all(post.reshape(count, count * count, 1, cells), 'vel', split...  17 us
    all_to_all x1, blocking collectives, local(): lax.all_to_all(state, 'vel', split_axis=2, concat_axis=1, tiled=True)  16.8 us
    dot_general x6, matrix products, inverse(): jnp.einsum(FORMS[2], cosine, second_real, precision=HIGHEST)  15.5 us
    dot_general x6, matrix products, inverse(): jnp.einsum(FORMS[2], sine_table, second_imag, precision=HIGHEST)  15 us
  transfers between devices with their start and end apart: 4, of which 2 were waited for; matrix products, arithmetic and copies ran while one was open for 7% of the time, Pallas kernels for 0%

commit v1 on v0

--- a/solution.py
+++ b/solution.py
@@ -231,7 +231,9 @@
             tiled=True,
         )
         center = back.reshape(local_y * local_xz, total_cells)
-        flux = lax.psum(jnp.dot(weights, center, precision=HIGHEST), ("vel", "sub"))
+        flux = jnp.sum(
+            lax.all_gather(jnp.dot(weights, center, precision=HIGHEST), ("vel", "sub")), axis=0
+        )
         shaped = center.reshape(local_y, local_xz, total_cells)
         bottom_rows = jnp.take(shaped, bottom_index, axis=2)
         top_rows = shaped[:, :, height_count - 1 :: height_count]

time: 535 us -> 511 us (0.955)
  blocking collectives: 116 us -> 97.3 us
    psum x2 -> x0, blocking collectives: 60.4 us -> none  [local(): flux = lax.psum(jnp.dot(weights, center, precision=HIGHEST), ('vel', 'sub'))]
    all_gather x0 -> x2, blocking collectives: none -> 41.8 us  [local(): lax.all_gather(jnp.dot(weights, center, precision=HIGHEST), ('vel', 'sub'))]
where the time goes in v1:
time: 511 us; the launch traced here: 506 us
  matrix products  244 us (48%)
  blocking collectives  97.3 us (19%)
  local copies, waits for them, and re-layouts  86.8 us (17%)
  other arithmetic  54.1 us (11%)
  waiting for transfers between devices  11.5 us (2%)
  starting transfers between devices  10.6 us (2%)
    dot_general x68, matrix products, apply(): return jnp.einsum(form, table, values, precision=HIGHEST)  212 us
    all_gather x2, blocking collectives, local(): lax.all_gather(jnp.dot(weights, center, precision=HIGHEST), ('vel', 'sub'))  41.8 us
    unnamed x83, local copies, waits for them, and re-layouts  20 us
    add x2, other arithmetic, collide(): return cube + rate * (gain - cube * inverse(tables[2]))  17.1 us
    all_to_all x1, blocking collectives, local(): lax.all_to_all(post.reshape(count, count * count, 1, cells), 'vel', split...  17 us
    all_to_all x1, blocking collectives, local(): lax.all_to_all(state, 'vel', split_axis=2, concat_axis=1, tiled=True)  16.5 us
    dot_general x6, matrix products, inverse(): jnp.einsum(FORMS[2], cosine, second_real, precision=HIGHEST)  15.5 us
    dot_general x6, matrix products, inverse(): jnp.einsum(FORMS[2], sine_table, second_imag, precision=HIGHEST)  15 us
  transfers between devices with their start and end apart: 4, of which 2 were waited for; matrix products, arithmetic and copies ran while one was open for 7% of the time, Pallas kernels for 0%

profile of v1, /device:TPU:1, one launch (start us, length us, event | category | flops | bytes accessed | tf_op | source)
XLA Modules:
  0.0 505.7 jit_solution(16626522347718903397)
XLA Ops:
  3.6 6.4 %all-to-all-start = ((f32[8,1,16384]{2,1,0:T(1,128)}), f32[8,1,16384]{2,1,0:T(1,128)S(1)}, u32[]{:S(2)}, u32[]{:S(2)}) async-start(f32[8,1,16384]{2,1,0:T(1,128)} %reshape.621), calls=%async_computation | async-start | bytes 1048576 | tf_op jit(solution)/shard_map/all_to_all | solution.py:210
  19.5 3.9 all-to-all-done
  27.4 5.8 %all_to_all.132 = f32[8,256,64]{1,0,2:T(8,128)S(1)} all-to-all(f32[8,256,64]{1,0,2:T(8,128)S(1)} %copy.780), channel_id=1, replica_groups=mesh['groups'=2,'vel'=8,'sub'=2] {'sub'}, dimensions={2} | all-to-all | bytes 1048576 | tf_op jit(solution)/shard_map/all_to_all | solution.py:209
  38.6 3.3 fusion.158
  41.9 3.3 fusion.160
  45.2 3.5 subtract_bitcast_fusion.7
  53.7 3.4 add_bitcast_fusion.7
  60.0 3.4 multiply_bitcast_fusion.10
  72.4 3.4 fusion.134
  75.8 3.3 fusion.136
  88.1 3.4 fusion.102
  91.4 3.7 fusion.104
  103.9 3.5 fusion.118
  107.4 3.3 fusion.120
  113.7 3.3 subtract_bitcast_fusion.6
  117.1 3.5 add_bitcast_fusion.6
  128.6 3.8 subtract_bitcast_fusion.4
  132.4 3.4 add_bitcast_fusion.4
  144.0 3.4 subtract_bitcast_fusion.5
  147.4 3.3 add_bitcast_fusion.5
  155.9 8.6 %fusion.5 = f32[16,16,16,32]{3,0,2,1:T(8,128)} fusion(f32[16,16,16,32]{3,0,2,1:T(8,128)S(1)} %bitcast.352, f32[16,16,32,16]{2,3,1,0:T(8,128)S(1)} %fusion.23, f32[16,16,32,16]{2,3,1,0:T(8,128)S(1)} %fusion.25, f32[16,16,32,16]{2,3,1,0:T(8,128)S(1)} %fusion.29, f32[16,16,32,16]{2,3,1,0:T(8,128)S(1)} %fusion.31, f32[16,16,32,16]{2,3,1,0:T(8,128)S(1)} %fusion.34, ...), kind=kLoop, calls=%fused_computation.9 | loop fusion | flops 1441792 | bytes 4194304 | tf_op jit(solution)/shard_map/add | solution.py:178
  167.7 3.9 all-to-all-start.2
  177.5 7.6 %all-to-all-done.2 = f32[8,1,16384]{2,1,0:T(1,128)S(1)} async-done(((f32[8,1,16384]{2,1,0:T(1,128)}), f32[8,1,16384]{2,1,0:T(1,128)S(1)}, u32[]{:S(2)}, u32[]{:S(2)}) %all-to-all-start.2) | async-done | bytes 524320 | tf_op jit(solution)/shard_map/all_to_all | solution.py:221
  192.3 5.5 %all_to_all.133 = f32[2,1,65536]{2,1,0:T(1,128)S(1)} all-to-all(f32[2,1,65536]{2,1,0:T(1,128)S(1)} %reshape.625), channel_id=1, replica_groups=mesh['groups'=2,'vel'=8,'sub'=2] {'sub'}, dimensions={0} | all-to-all | bytes 1048576 | tf_op jit(solution)/shard_map/all_to_all | solution.py:220
  217.3 21.6 %all-gather.2 = f32[16,4,512]{2,1,0:T(4,128)} all-gather(f32[1,4,512]{2,1,0:T(4,128)S(1)} %convolution_bitcast_fusion.1), channel_id=2, replica_groups=mesh['groups'=2,'vel'=8,'sub'=2] {'vel','sub'}, dimensions={0}, use_global_device_ids=true | all-gather | bytes 139264 | tf_op jit(solution)/shard_map/all_gather | solution.py:235
  243.3 3.9 slice_divide_fusion.5
  257.9 3.3 fusion.253
  263.9 16.5 %all_to_all.134 = f32[8,1,16384]{2,1,0:T(1,128)S(1)} all-to-all(f32[8,1,16384]{2,1,0:T(1,128)S(1)} %reshape.627), channel_id=1, replica_groups=mesh['groups'=2,'vel'=8,'sub'=2] {'vel'}, dimensions={0} | all-to-all | bytes 1048576 | tf_op jit(solution)/shard_map/all_to_all | solution.py:210
  284.0 5.1 %all_to_all.135 = f32[8,256,64]{1,0,2:T(8,128)S(1)} all-to-all(f32[8,256,64]{1,0,2:T(8,128)S(1)} %copy.847), channel_id=1, replica_groups=mesh['groups'=2,'vel'=8,'sub'=2] {'sub'}, dimensions={2} | all-to-all | bytes 1048576 | tf_op jit(solution)/shard_map/all_to_all | solution.py:209
  294.5 3.4 fusion.94
  301.1 3.7 subtract_bitcast_fusion.3
  309.8 3.4 add_bitcast_fusion.3
  315.9 3.4 multiply_bitcast_fusion.4
  328.3 3.3 fusion.70
  337.9 3.3 fusion.48
  344.1 3.3 fusion.38
  347.5 3.5 fusion.40
  359.7 3.6 fusion.54
  369.6 3.3 subtract_bitcast_fusion.2
  373.0 3.7 add_bitcast_fusion.2
  384.7 3.6 subtract_bitcast_fusion
  388.3 3.4 add_bitcast_fusion
  399.9 3.4 subtract_bitcast_fusion.1
  403.3 3.3 add_bitcast_fusion.1
  412.0 8.6 %fusion.2 = f32[16,16,16,32]{3,0,2,1:T(8,128)} fusion(f32[16,16,16,32]{3,0,2,1:T(8,128)S(1)} %bitcast.349, f32[16,16,32,16]{2,3,1,0:T(8,128)S(1)} %fusion.7, f32[16,16,32,16]{2,3,1,0:T(8,128)S(1)} %fusion.9, f32[16,16,32,16]{2,3,1,0:T(8,128)S(1)} %fusion.13, f32[16,16,32,16]{2,3,1,0:T(8,128)S(1)} %fusion.15, f32[16,16,32,16]{2,3,1,0:T(8,128)S(1)} %fusion.18, ...), kind=kLoop, calls=%fused_computation.5 | loop fusion | flops 1441792 | bytes 4194304 | tf_op jit(solution)/shard_map/add | solution.py:178
  423.0 17.0 %all_to_all.136 = f32[8,1,16384]{2,1,0:T(1,128)S(1)} all-to-all(f32[8,1,16384]{2,1,0:T(1,128)S(1)} %reshape.629), channel_id=1, replica_groups=mesh['groups'=2,'vel'=8,'sub'=2] {'vel'}, dimensions={0} | all-to-all | bytes 1048576 | tf_op jit(solution)/shard_map/all_to_all | solution.py:221
  447.1 5.5 %all_to_all.137 = f32[2,1,65536]{2,1,0:T(1,128)S(1)} all-to-all(f32[2,1,65536]{2,1,0:T(1,128)S(1)} %reshape.631), channel_id=1, replica_groups=mesh['groups'=2,'vel'=8,'sub'=2] {'sub'}, dimensions={0} | all-to-all | bytes 1048576 | tf_op jit(solution)/shard_map/all_to_all | solution.py:220
  470.3 20.2 %all-gather.3 = f32[16,4,512]{2,1,0:T(4,128)S(1)} all-gather(f32[1,4,512]{2,1,0:T(4,128)S(1)} %convolution_bitcast_fusion), channel_id=3, replica_groups=mesh['groups'=2,'vel'=8,'sub'=2] {'vel','sub'}, dimensions={0}, use_global_device_ids=true | all-gather | bytes 139264 | tf_op jit(solution)/shard_map/all_gather | solution.py:235
  (245 shorter events, 250.9 us)
Async XLA Ops:
  1.8 11.1 %copy-start.33 = (s32[32]{0:T(128)S(1)}, s32[32]{0:T(128)}, u32[]{:S(2)}) copy-start(s32[32]{0:T(128)} %param.7) | copy-start | bytes 388
  1.8 11.1 %copy-start.12 = (s32[512]{0:T(512)S(1)}, s32[512]{0:T(512)}, u32[]{:S(2)}) copy-start(s32[512]{0:T(512)} %param.6) | copy-start | bytes 6148
  3.6 19.8 %all-to-all-start = ((f32[8,1,16384]{2,1,0:T(1,128)}), f32[8,1,16384]{2,1,0:T(1,128)S(1)}, u32[]{:S(2)}, u32[]{:S(2)}) async-start(f32[8,1,16384]{2,1,0:T(1,128)} %reshape.621), calls=%async_computation | async-start | bytes 1048576 | tf_op jit(solution)/shard_map/all_to_all | solution.py:210
  10.5 8.9 %copy-start.23 = (f32[8]{0:T(128)}, f32[8]{0:T(128)S(1)}, u32[]{:S(2)}) copy-start(f32[8]{0:T(128)S(1)} %get-tuple-element.71) | copy-start | bytes 100
  12.9 6.5 %copy-start.24 = (f32[32]{0:T(128)}, f32[32]{0:T(128)S(1)}, u32[]{:S(2)}) copy-start(f32[32]{0:T(128)S(1)} %get-tuple-element.67) | copy-start | bytes 388
  17.3 240.5 %copy-start.13 = (f32[512]{0:T(512)}, f32[512]{0:T(512)S(1)}, u32[]{:S(2)}) copy-start(f32[512]{0:T(512)S(1)} %sub.287) | copy-start | bytes 6148
  164.5 9.8 %copy-start.21 = (f32[496]{0:T(512)S(1)}, f32[496]{0:T(512)}, u32[]{:S(2)}) copy-start(f32[496]{0:T(512)} %get-tuple-element.55) | copy-start | bytes 5956
  164.5 9.8 %copy-start.22 = (f32[496]{0:T(512)S(1)}, f32[496]{0:T(512)}, u32[]{:S(2)}) copy-start(f32[496]{0:T(512)} %get-tuple-element.56) | copy-start | bytes 5956
  164.5 9.8 %copy-start.26 = (f32[16]{0:T(128)S(1)}, f32[16]{0:T(128)}, u32[]{:S(2)}) copy-start(f32[16]{0:T(128)} %get-tuple-element.53) | copy-start | bytes 196
  164.5 9.8 %copy-start.27 = (f32[16]{0:T(128)S(1)}, f32[16]{0:T(128)}, u32[]{:S(2)}) copy-start(f32[16]{0:T(128)} %get-tuple-element.54) | copy-start | bytes 196
  164.5 10.5 %copy-start.32 = (s32[32]{0:T(128)S(1)}, s32[32]{0:T(128)}, u32[]{:S(2)}) copy-start(s32[32]{0:T(128)} %get-tuple-element.11) | copy-start | bytes 388
  164.5 12.9 %copy-start.28 = (f32[8]{0:T(128)S(1)}, f32[8]{0:T(128)}, u32[]{:S(2)}) copy-start(f32[8]{0:T(128)} %get-tuple-element.72) | copy-start | bytes 100
  164.5 12.9 %copy-start.29 = (f32[32]{0:T(128)S(1)}, f32[32]{0:T(128)}, u32[]{:S(2)}) copy-start(f32[32]{0:T(128)} %get-tuple-element.63) | copy-start | bytes 388
  164.5 12.9 %copy-start.30 = (f32[32]{0:T(128)S(1)}, f32[32]{0:T(128)}, u32[]{:S(2)}) copy-start(f32[32]{0:T(128)} %get-tuple-element.64) | copy-start | bytes 388
  164.6 12.9 %copy-start.31 = (f32[32]{0:T(128)S(1)}, f32[32]{0:T(128)}, u32[]{:S(2)}) copy-start(f32[32]{0:T(128)} %get-tuple-element.68) | copy-start | bytes 388
  167.7 17.5 %all-to-all-start.2 = ((f32[8,1,16384]{2,1,0:T(1,128)}), f32[8,1,16384]{2,1,0:T(1,128)S(1)}, u32[]{:S(2)}, u32[]{:S(2)}) async-start(f32[8,1,16384]{2,1,0:T(1,128)} %reshape.623), calls=%async_computation.2 | async-start | bytes 1048576 | tf_op jit(solution)/shard_map/all_to_all | solution.py:221
  177.5 80.3 %copy-start.8 = (f32[8,32]{1,0:T(8,128)}, f32[8,32]{1,0:T(8,128)S(1)}, u32[]{:S(2)}) copy-start(f32[8,32]{1,0:T(8,128)S(1)} %get-tuple-element.57) | copy-start | bytes 3076
  177.5 80.3 %copy-start.10 = (f32[8,32]{1,0:T(8,128)}, f32[8,32]{1,0:T(8,128)S(1)}, u32[]{:S(2)}) copy-start(f32[8,32]{1,0:T(8,128)S(1)} %get-tuple-element.58) | copy-start | bytes 3076
  208.0 2.7 copy-start.1
  240.2 13.7 %copy-start.7 = (f32[256,496]{0,1:T(8,128)S(1)}, f32[256,496]{0,1:T(8,128)}, u32[]{:S(2)}) copy-start(f32[256,496]{0,1:T(8,128)} %get-tuple-element.33) | copy-start | bytes 1523716
  240.2 14.7 %copy-start.5 = (f32[256,511]{0,1:T(8,128)S(1)}, f32[256,511]{0,1:T(8,128)}, u32[]{:S(2)}) copy-start(f32[256,511]{0,1:T(8,128)} %get-tuple-element.30) | copy-start | bytes 1569796
  241.3 14.6 %copy-start.4 = (f32[256,511]{0,1:T(8,128)S(1)}, f32[256,511]{0,1:T(8,128)}, u32[]{:S(2)}) copy-start(f32[256,511]{0,1:T(8,128)} %get-tuple-element.31) | copy-start | bytes 1569796
  242.3 14.7 %collective-permute-start = (f32[8,32,32]{2,1,0:T(8,128)S(1)}, f32[8,32,32]{2,1,0:T(8,128)S(1)}, u32[]{:S(2)}, u32[]{:S(2)}) collective-permute-start(f32[8,32,32]{2,1,0:T(8,128)S(1)} %bitcast_select_fusion.1), channel_id=1, source_target_pairs={{0,1},{1,0},{2,3},{3,2},{4,5},{5,4},{6,7},{7,6},{8,9},{9,8},{10,11... | collective-permute-start | bytes 98312 | tf_op jit(solution)/shard_map/ppermute | solution.py:22
  460.8 2.2 copy-start.17
  460.8 2.2 copy-start.18
  460.8 2.2 copy-start.19
  460.8 2.2 copy-start.20
  463.5 2.1 copy-start
  468.3 22.4 %copy-start.16 = (f32[1,512]{1,0:T(1,128)S(1)}, f32[1,512]{1,0:T(1,128)}, u32[]{:S(2)}) copy-start(f32[1,512]{1,0:T(1,128)} %stack_reshape.3) | copy-start | bytes 6148
  468.3 26.4 %copy-start.25 = (pred[32]{0:T(512)(128)(4,1)S(1)}, pred[32]{0:T(512)(128)(4,1)}, u32[]{:S(2)}) copy-start(pred[32]{0:T(512)(128)(4,1)} %get-tuple-element.10) | copy-start | bytes 100
  494.6 3.7 copy-start.6
  494.6 4.7 copy-start.3
  494.7 5.6 %copy-start.2 = (f32[256,511]{0,1:T(8,128)S(1)}, f32[256,511]{0,1:T(8,128)}, u32[]{:S(2)}) copy-start(f32[256,511]{0,1:T(8,128)} %get-tuple-element.25) | copy-start | bytes 1569796
  494.8 6.6 %collective-permute-start.1 = (f32[8,32,32]{2,1,0:T(8,128)S(1)}, f32[8,32,32]{2,1,0:T(8,128)S(1)}, u32[]{:S(2)}, u32[]{:S(2)}) collective-permute-start(f32[8,32,32]{2,1,0:T(8,128)S(1)} %bitcast_select_fusion), channel_id=1, source_target_pairs={{0,1},{1,0},{2,3},{3,2},{4,5},{5,4},{6,7},{7,6},{8,9},{9,8},{10,11... | collective-permute-start | bytes 98312 | tf_op jit(solution)/shard_map/ppermute | solution.py:22
  501.5 0.8 copy-start.9
  501.5 0.8 copy-start.11
  501.5 0.8 copy-start.14
  501.5 0.8 copy-start.15
